TPU v7x, 512 devices: a whole 4x8x8 slice. The times are simulated.
512 devices in a mesh: dp: 16 (over z, y_hi), seq: 8 (over y_lo, core), tensor: 4 (over x).
Axes of the slice: x: 4, y: 8 (y_hi: 2, y_lo: 4; y = y_hi * 4 + y_lo), z: 8, core: 2. Of those that a mesh axis runs over, the one named last changes fastest.
Arguments:
- activations: bfloat16 [32768, 512], P(('dp', 'seq')), may hold values from -6 to 6
- d_logits: bfloat16 [32768, 8192], P(('dp', 'seq'), 'tensor'), may hold values from -0.015625 to 0.015625
- block_owner: int32 [16], replicated, may hold values from 0 to 15, each once
- left_stat: float32 [16, 512, 512], P('dp', ('seq', 'tensor')), may hold values from -0.1 to 2.1
- right_stat: float32 [16, 512, 512], P('dp', ('seq', 'tensor')), may hold values from -0.1 to 2.1
- second_moment: float32 [16, 512, 512], P('dp', ('seq', 'tensor')), may hold values from 2e-05 to 0.002
- left_root: float32 [16, 512, 512], P('dp', ('seq', 'tensor')), may hold values from -0.15 to 14
- right_root: float32 [16, 512, 512], P('dp', ('seq', 'tensor')), may hold values from -0.15 to 14
Outputs:
- update: bfloat16 [16, 512, 512], P(None, ('seq', 'tensor'))
- left_new: float32 [16, 512, 512], P('dp', ('seq', 'tensor'))
- right_new: float32 [16, 512, 512], P('dp', ('seq', 'tensor'))
- moment_new: float32 [16, 512, 512], P('dp', ('seq', 'tensor'))
All inputs are finite; a program needn't handle non-finite values.
Results may differ from a plain program's by a relative error of at most 0.00055.
Values may be sent and summed in bfloat16 or wider, within the bound.
A program may use at most 64 MiB of HBM per device.

v0:
```python
import jax
import jax.numpy as jnp
from jax import lax
from jax.sharding import PartitionSpec as P

highest = lax.Precision.HIGHEST


def gradient_rows(logit_columns, activations):
    return lax.dot_general(
        logit_columns, activations, (((0,), (0,)), ((), ())), preferred_element_type=jnp.float32
    )


def per_device(
    activations, d_logits, block_owner, left_stat, right_stat, second_moment, left_root, right_root
):
    tokens_here = d_logits.shape[0]
    block_count = block_owner.shape[0]
    block_width = activations.shape[1]
    seq_count = lax.axis_size("seq")
    tensor_count = lax.axis_size("tensor")
    row_share = block_width // (seq_count * tensor_count)
    block_band = block_width // tensor_count
    indices = jnp.arange(block_count, dtype=jnp.int32)
    matches = block_owner[None, :] == indices[:, None]
    owner_block = jnp.sum(jnp.where(matches, indices[None, :], 0), axis=1)
    by_owner = jnp.take(d_logits.reshape(tokens_here, block_count, block_band), owner_block, axis=1)
    by_owner = by_owner.reshape(tokens_here, block_count * block_band)
    grad_slab = lax.psum_scatter(
        gradient_rows(by_owner, activations), ("dp", "seq"), scatter_dimension=0, tiled=True
    )
    moment_next = 0.99 * second_moment[0] + 0.01 * grad_slab * grad_slab
    adam_dir = grad_slab / (jnp.sqrt(moment_next) + 1e-08)
    adam_part = jnp.sum(adam_dir * adam_dir)
    adam_total = lax.psum(adam_part, ("seq", "tensor"))
    first_row = (lax.axis_index("seq") * tensor_count + lax.axis_index("tensor")) * row_share
    left_rows = left_root[0]
    slab_rows = lax.all_gather(grad_slab, ("seq", "tensor"), axis=0, tiled=True)
    outer_rows = jnp.dot(
        grad_slab, slab_rows.T, precision=highest, preferred_element_type=jnp.float32
    )
    own_columns = lax.dynamic_slice_in_dim(slab_rows, first_row, row_share, 1)
    right_part = jnp.dot(
        own_columns.T, slab_rows, precision=highest, preferred_element_type=jnp.float32
    )
    mixed_part = jnp.dot(
        left_rows, slab_rows, precision=highest, preferred_element_type=jnp.float32
    )
    left_next = 0.95 * left_stat[0] + outer_rows
    right_next = 0.95 * right_stat[0] + right_part
    precond = jnp.dot(
        mixed_part,
        lax.all_gather(right_root[0], ("seq", "tensor"), axis=0, tiled=True),
        precision=highest,
        preferred_element_type=jnp.float32,
    )
    precond_part = jnp.sum(precond * precond)
    precond_total = lax.psum(precond_part, ("seq", "tensor"))
    graft_scale = jnp.sqrt(adam_total) / (jnp.sqrt(precond_total) + 1e-06)
    update_rows = (graft_scale * precond).astype(jnp.bfloat16)
    gathered = lax.all_gather(update_rows[None], "dp", axis=0, tiled=True)
    update = jnp.take(gathered, block_owner, axis=0)
    return (update, left_next[None], right_next[None], moment_next[None])


def solution(mesh):
    return jax.shard_map(
        per_device,
        mesh=mesh,
        in_specs=(
            P(("dp", "seq"), None),
            P(("dp", "seq"), "tensor"),
            P(),
            P("dp", ("seq", "tensor"), None),
            P("dp", ("seq", "tensor"), None),
            P("dp", ("seq", "tensor"), None),
            P("dp", ("seq", "tensor"), None),
            P("dp", ("seq", "tensor"), None),
        ),
        out_specs=(
            P(None, ("seq", "tensor"), None),
            P("dp", ("seq", "tensor"), None),
            P("dp", ("seq", "tensor"), None),
            P("dp", ("seq", "tensor"), None),
        ),
        check_vma=False,
    )
```

profile of v0, /device:TPU:2, one launch (start us, length us, event | category | flops | bytes accessed | tf_op | source)
XLA Modules:
  0.0 537.0 jit_solution(10897611241762053604)
XLA Ops:
  7.2 0.0 copy-start
  7.2 0.0 reduce-scatter.2.cloned.1.call-start
  7.2 0.8 select_reduce_fusion
  8.1 1.5 copy.15
  9.6 0.7 copy.16
  10.2 0.7 gather_fusion
  11.0 0.5 copy.17
  11.5 0.1 broadcast_bitcast_fusion
  11.6 0.5 bitcast_select_fusion
  12.1 0.0 copy-done
  12.1 2.6 fusion.11
  14.8 0.0 copy-start.6
  14.8 0.0 copy-start.2
  14.8 0.0 copy-start.3
  14.8 0.0 copy-start.4
  14.8 0.0 copy-start.5
  14.8 0.0 reduce-scatter.2.cloned.1.call-update
  14.8 0.0 all-gather.5.cloned.1.call-start
  14.9 206.3 %reduce-scatter.2.cloned.1.call-done = f32[16,512]{1,0:T(8,128)} async-done(((f32[2048,512]{1,0:T(8,128)}), f32[16,512]{1,0:T(8,128)}) %reduce-scatter.2.cloned.1.call-update) | async-done | bytes 32784 | tf_op jit(solution)/shard_map/reduce_scatter | solution.py:30
  221.1 0.0 all-gather.5.cloned.1.call-update
  221.2 0.0 all-gather.7.cloned.1.call-start
  221.2 0.7 all-gather.7.cloned.1.call-update
  221.9 0.0 copy-done.6
  222.0 0.0 copy-done.2
  222.0 2.0 fusion.8
  224.0 83.4 %all-gather.5.cloned.1.call-done = f32[512,512]{1,0:T(8,128)} async-done(((f32[16,512]{1,0:T(8,128)}), f32[512,512]{1,0:T(8,128)}) %all-gather.5.cloned.1.call-update) | async-done | bytes 1048592 | tf_op jit(solution)/shard_map/all_gather | solution.py:39
  307.3 0.0 copy-done.3
  307.3 0.0 copy-start.1
  307.3 2.0 fusion.6
  309.3 87.3 %all-gather.7.cloned.1.call-done = f32[1,512,512]{2,1,0:T(8,128)} async-done(((f32[1,16,512]{2,1,0:T(8,128)}), f32[1,512,512]{2,1,0:T(8,128)}) %all-gather.7.cloned.1.call-update) | async-done | bytes 1048592 | tf_op jit(solution)/shard_map/all_gather | solution.py:54
  396.6 2.4 multiply_reduce_fusion
  399.1 69.5 %all-reduce = (f32[]{:T(128)}, f32[]{:T(128)}) all-reduce(f32[]{:T(128)} %get-tuple-element.7, f32[]{:T(128)} %get-tuple-element.8), channel_id=1, replica_groups=mesh['dp'=16,'seq'=8,'tensor'=4] {'seq','tensor'}, use_global_device_ids=true, to_apply=%region_3.4 | all-reduce | flops 2 | bytes 16 | tf_op jit(solution)/shard_map/psum | solution.py:36
  470.0 55.5 %all-gather.1 = bf16[256,512]{1,0:T(8,128)(2,1)S(1)} all-gather(bf16[16,512]{1,0:T(8,128)(2,1)S(1)} %multiply_convert_fusion), channel_id=3, replica_groups=mesh['dp'=16,'seq'=8,'tensor'=4] {'dp'}, dimensions={0}, use_global_device_ids=true | all-gather | bytes 278528 | tf_op jit(solution)/shard_map/all_gather | solution.py:62
  525.5 0.6 gather_fusion.1
  526.0 0.8 broadcast_select_fusion
  526.8 0.0 copy-done.4
  526.8 0.0 copy-done.1
  526.8 2.3 fusion
  529.2 0.0 copy-done.5
  529.2 1.3 fusion.1
  (7 shorter events, 0.0 us)
Async XLA Ops:
  7.2 5.0 copy-start
  7.2 214.0 %reduce-scatter.2.cloned.1.call-start = ((), (), s32[]{:S(2)}) async-start(), calls=%async_computation.1 | async-start | bytes 4227072 | tf_op jit(solution)/shard_map/reduce_scatter | solution.py:30
  14.8 207.1 %copy-start.6 = (s32[16]{0:T(128)S(1)}, s32[16]{0:T(128)}, u32[]{:S(2)}) copy-start(s32[16]{0:T(128)} %param.10) | copy-start | bytes 196
  14.8 207.2 %copy-start.2 = (f32[1,16,512]{2,1,0:T(8,128)S(1)}, f32[1,16,512]{2,1,0:T(8,128)}, u32[]{:S(2)}) copy-start(f32[1,16,512]{2,1,0:T(8,128)} %param.13) | copy-start | bytes 98308
  14.8 292.6 %copy-start.3 = (f32[1,16,512]{2,1,0:T(8,128)S(1)}, f32[1,16,512]{2,1,0:T(8,128)}, u32[]{:S(2)}) copy-start(f32[1,16,512]{2,1,0:T(8,128)} %param.14) | copy-start | bytes 98308
  14.8 512.1 %copy-start.4 = (f32[1,16,512]{2,1,0:T(8,128)S(1)}, f32[1,16,512]{2,1,0:T(8,128)}, u32[]{:S(2)}) copy-start(f32[1,16,512]{2,1,0:T(8,128)} %param.11) | copy-start | bytes 98308
  14.8 514.4 %copy-start.5 = (f32[1,16,512]{2,1,0:T(8,128)S(1)}, f32[1,16,512]{2,1,0:T(8,128)}, u32[]{:S(2)}) copy-start(f32[1,16,512]{2,1,0:T(8,128)} %param.12) | copy-start | bytes 98308
  14.8 292.5 %all-gather.5.cloned.1.call-start = ((), (), s32[]{:S(2)}) async-start(), calls=%async_computation.2 | async-start | bytes 1081344 | tf_op jit(solution)/shard_map/all_gather | solution.py:39
  221.2 175.4 %all-gather.7.cloned.1.call-start = ((), (), s32[]{:S(2)}) async-start(), calls=%async_computation.3 | async-start | bytes 1081344 | tf_op jit(solution)/shard_map/all_gather | solution.py:54
  307.3 219.5 %copy-start.1 = (f32[512,512]{1,0:T(8,128)S(1)}, f32[512,512]{1,0:T(8,128)}, u32[]{:S(2)}) copy-start(f32[512,512]{1,0:T(8,128)} %all-gather.5.cloned.1.call-done) | copy-start | bytes 3145732
Sparse Core Ops, SparseCore 0:
  14.9 206.1 reduce-scatter.1
  223.5 83.8 all-gather.4
  309.7 86.9 all-gather.6
where the time goes:
time: 537 us
  waiting for transfers between devices  378 us (70%)
  blocking collectives  125 us (23%)
  between operations  15.3 us (3%)
  matrix products  10.7 us (2%)
    reduce_scatter x1, waiting for transfers between devices, per_device(): lax.psum_scatter(gradient_rows(by_owner, activations), ('dp', 'seq'), sca...  206 us
    all_gather x1, waiting for transfers between devices, per_device(): lax.all_gather(right_root[0], ('seq', 'tensor'), axis=0, tiled=True)  87.3 us
    all_gather x1, waiting for transfers between devices, per_device(): slab_rows = lax.all_gather(grad_slab, ('seq', 'tensor'), axis=0, tiled=True)  83.4 us
    psum x1, blocking collectives, per_device(): adam_total = lax.psum(adam_part, ('seq', 'tensor'))  69.5 us
    all_gather x1, blocking collectives, per_device(): gathered = lax.all_gather(update_rows[None], 'dp', axis=0, tiled=True)  55.5 us
  transfers between devices with their start and end apart: 3, of which 3 were waited for; matrix products, arithmetic and copies ran while one was open for 1% of the time, Pallas kernels for 0%

commit v1 on v0

--- a/solution.py
+++ b/solution.py
@@ -59,7 +59,9 @@
     precond_total = lax.psum(precond_part, ("seq", "tensor"))
     graft_scale = jnp.sqrt(adam_total) / (jnp.sqrt(precond_total) + 1e-06)
     update_rows = (graft_scale * precond).astype(jnp.bfloat16)
-    gathered = lax.all_gather(update_rows[None], "dp", axis=0, tiled=True)
+    gathered = jnp.concatenate(
+        lax.all_to_all(jnp.stack([update_rows[None]] * lax.axis_size("dp")), "dp", 0, 0), axis=0
+    )
     update = jnp.take(gathered, block_owner, axis=0)
     return (update, left_next[None], right_next[None], moment_next[None])
 

time: 537 us -> 504 us (0.939)
  the two profiles are of different devices: /device:TPU:2 before, /device:TPU:64 now
where the time goes in v1:
time: 504 us
  waiting for transfers between devices  385 us (76%)
  blocking collectives  72.7 us (14%)
  between operations  15.3 us (3%)
  matrix products  11.3 us (2%)
  starting transfers between devices  10.5 us (2%)
    reduce_scatter x1, waiting for transfers between devices, per_device(): lax.psum_scatter(gradient_rows(by_owner, activations), ('dp', 'seq'), sca...  204 us
    all_gather x1, waiting for transfers between devices, per_device(): lax.all_gather(right_root[0], ('seq', 'tensor'), axis=0, tiled=True)  87.3 us
    all_gather x1, waiting for transfers between devices, per_device(): slab_rows = lax.all_gather(grad_slab, ('seq', 'tensor'), axis=0, tiled=True)  84.6 us
    psum x1, blocking collectives, per_device(): adam_total = lax.psum(adam_part, ('seq', 'tensor'))  72.7 us
    all_to_all x1, starting transfers between devices, per_device(): lax.all_to_all(jnp.stack([update_rows[None]] * lax.axis_size('dp')), 'dp'...  10.3 us
  transfers between devices with their start and end apart: 4, of which 4 were waited for; matrix products, arithmetic and copies ran while one was open for 2% of the time, Pallas kernels for 0%

profile of v1, /device:TPU:64, one launch (start us, length us, event | category | flops | bytes accessed | tf_op | source)
XLA Modules:
  0.0 503.7 jit_solution(6059647440261891193)
XLA Ops:
  7.2 0.0 copy-start
  7.2 0.0 reduce-scatter.2.cloned.1.call-start
  7.2 0.8 select_reduce_fusion
  8.1 1.5 copy.18
  9.6 0.7 copy.19
  10.2 0.7 gather_fusion
  11.0 0.5 copy.20
  11.5 0.1 broadcast_bitcast_fusion
  11.6 0.5 bitcast_select_fusion
  12.1 0.0 copy-done
  12.1 2.6 fusion.11
  14.8 0.0 copy-start.7
  14.8 0.0 copy-start.3
  14.8 0.0 copy-start.4
  14.8 0.0 copy-start.5
  14.8 0.0 copy-start.6
  14.8 0.0 reduce-scatter.2.cloned.1.call-update
  14.8 0.0 all-gather.4.cloned.1.call-start
  14.9 204.5 %reduce-scatter.2.cloned.1.call-done = f32[16,512]{1,0:T(8,128)} async-done(((f32[2048,512]{1,0:T(8,128)}), f32[16,512]{1,0:T(8,128)}) %reduce-scatter.2.cloned.1.call-update) | async-done | bytes 32784 | tf_op jit(solution)/shard_map/reduce_scatter | solution.py:30
  219.3 0.0 copy-start.2
  219.3 0.0 all-gather.4.cloned.1.call-update
  219.4 0.0 all-gather.6.cloned.1.call-start
  219.4 0.7 all-gather.6.cloned.1.call-update
  220.1 0.0 copy-done.7
  220.1 0.0 copy-done.3
  220.1 2.0 fusion.8
  222.1 84.6 %all-gather.4.cloned.1.call-done = f32[512,512]{1,0:T(8,128)} async-done(((f32[16,512]{1,0:T(8,128)}), f32[512,512]{1,0:T(8,128)}) %all-gather.4.cloned.1.call-update) | async-done | bytes 1048592 | tf_op jit(solution)/shard_map/all_gather | solution.py:39
  306.7 0.0 copy-done.4
  306.7 0.0 copy-start.1
  306.7 2.0 fusion.6
  308.6 87.3 %all-gather.6.cloned.1.call-done = f32[1,512,512]{2,1,0:T(8,128)} async-done(((f32[1,16,512]{2,1,0:T(8,128)}), f32[1,512,512]{2,1,0:T(8,128)}) %all-gather.6.cloned.1.call-update) | async-done | bytes 1048592 | tf_op jit(solution)/shard_map/all_gather | solution.py:54
  395.9 2.4 multiply_reduce_fusion
  398.4 72.7 %all-reduce = (f32[]{:T(128)}, f32[]{:T(128)}) all-reduce(f32[]{:T(128)} %get-tuple-element.7, f32[]{:T(128)} %get-tuple-element.8), channel_id=1, replica_groups=mesh['dp'=16,'seq'=8,'tensor'=4] {'seq','tensor'}, use_global_device_ids=true, to_apply=%region_3.4 | all-reduce | flops 2 | bytes 16 | tf_op jit(solution)/shard_map/psum | solution.py:36
  472.5 0.7 stack.3
  473.3 10.3 %all-to-all-start = ((bf16[16,1,16,512]{3,2,1,0:T(8,128)(2,1)}), bf16[16,1,16,512]{3,2,1,0:T(8,128)(2,1)S(1)}, u32[]{:S(2)}, u32[]{:S(2)}) async-start(bf16[16,1,16,512]{3,2,1,0:T(8,128)(2,1)} %stack.3), calls=%async_computation.1 | async-start | bytes 524288 | tf_op jit(solution)/shard_map/all_to_all | solution.py:63
  483.6 0.0 copy-done.5
  483.6 2.6 fusion.1
  486.3 0.0 copy-done.6
  486.3 0.0 copy-done.2
  486.3 0.0 copy-done.1
  486.3 1.6 fusion
  487.9 7.9 %all-to-all-done = bf16[16,1,16,512]{3,2,1,0:T(8,128)(2,1)S(1)} async-done(((bf16[16,1,16,512]{3,2,1,0:T(8,128)(2,1)}), bf16[16,1,16,512]{3,2,1,0:T(8,128)(2,1)S(1)}, u32[]{:S(2)}, u32[]{:S(2)}) %all-to-all-start) | async-done | bytes 262176 | tf_op jit(solution)/shard_map/all_to_all | solution.py:63
  495.8 0.6 gather_fusion.1
  496.3 0.8 broadcast_select_fusion
  (7 shorter events, 0.0 us)
Async XLA Ops:
  7.2 5.0 copy-start
  7.2 212.1 %reduce-scatter.2.cloned.1.call-start = ((), (), s32[]{:S(2)}) async-start(), calls=%async_computation.2 | async-start | bytes 4227072 | tf_op jit(solution)/shard_map/reduce_scatter | solution.py:30
  14.8 205.3 %copy-start.7 = (s32[16]{0:T(128)S(1)}, s32[16]{0:T(128)}, u32[]{:S(2)}) copy-start(s32[16]{0:T(128)} %param.10) | copy-start | bytes 196
  14.8 205.4 %copy-start.3 = (f32[1,16,512]{2,1,0:T(8,128)S(1)}, f32[1,16,512]{2,1,0:T(8,128)}, u32[]{:S(2)}) copy-start(f32[1,16,512]{2,1,0:T(8,128)} %param.13) | copy-start | bytes 98308
  14.8 291.9 %copy-start.4 = (f32[1,16,512]{2,1,0:T(8,128)S(1)}, f32[1,16,512]{2,1,0:T(8,128)}, u32[]{:S(2)}) copy-start(f32[1,16,512]{2,1,0:T(8,128)} %param.14) | copy-start | bytes 98308
  14.8 468.8 %copy-start.5 = (f32[1,16,512]{2,1,0:T(8,128)S(1)}, f32[1,16,512]{2,1,0:T(8,128)}, u32[]{:S(2)}) copy-start(f32[1,16,512]{2,1,0:T(8,128)} %param.12) | copy-start | bytes 98308
  14.8 471.5 %copy-start.6 = (f32[1,16,512]{2,1,0:T(8,128)S(1)}, f32[1,16,512]{2,1,0:T(8,128)}, u32[]{:S(2)}) copy-start(f32[1,16,512]{2,1,0:T(8,128)} %param.11) | copy-start | bytes 98308
  14.8 291.9 %all-gather.4.cloned.1.call-start = ((), (), s32[]{:S(2)}) async-start(), calls=%async_computation.3 | async-start | bytes 1081344 | tf_op jit(solution)/shard_map/all_gather | solution.py:39
  219.3 266.9 %copy-start.2 = (f32[16,512]{1,0:T(8,128)S(1)}, f32[16,512]{1,0:T(8,128)}, u32[]{:S(2)}) copy-start(f32[16,512]{1,0:T(8,128)} %reduce-scatter.2.cloned.1.call-done) | copy-start | bytes 98308
  219.4 176.6 %all-gather.6.cloned.1.call-start = ((), (), s32[]{:S(2)}) async-start(), calls=%async_computation.4 | async-start | bytes 1081344 | tf_op jit(solution)/shard_map/all_gather | solution.py:54
  306.7 179.6 %copy-start.1 = (f32[512,512]{1,0:T(8,128)S(1)}, f32[512,512]{1,0:T(8,128)}, u32[]{:S(2)}) copy-start(f32[512,512]{1,0:T(8,128)} %all-gather.4.cloned.1.call-done) | copy-start | bytes 3145732
  473.3 22.5 %all-to-all-start = ((bf16[16,1,16,512]{3,2,1,0:T(8,128)(2,1)}), bf16[16,1,16,512]{3,2,1,0:T(8,128)(2,1)S(1)}, u32[]{:S(2)}, u32[]{:S(2)}) async-start(bf16[16,1,16,512]{3,2,1,0:T(8,128)(2,1)} %stack.3), calls=%async_computation.1 | async-start | bytes 524288 | tf_op jit(solution)/shard_map/all_to_all | solution.py:63
Sparse Core Ops, SparseCore 0:
  14.9 204.3 reduce-scatter.1
  221.6 84.9 all-gather.3
  309.0 86.9 all-gather.5
